TPU v7x, 32 devices: a whole 2x2x4 slice. The times are simulated.
32 devices in a mesh: rep: 2 (over x), feat: 16 (over z, y, core).
Axes of the slice: x: 2, y: 2, z: 4, core: 2. Of those that a mesh axis runs over, the one named last changes fastest.
Arguments:
- view_a: bfloat16 [512, 16384], P(('rep', 'feat')), parts along dimension 0, may hold values from -13 to 13
- view_b: bfloat16 [512, 16384], P(('rep', 'feat')), parts along dimension 0, may hold values from -13 to 13
Outputs:
- grad_a: bfloat16 [512, 16384], P(('rep', 'feat')), parts along dimension 0
- grad_b: bfloat16 [512, 16384], P(('rep', 'feat')), parts along dimension 0
There are 2 independent parts, one for each index of `rep`. A program takes and returns all parts, laid end to end along the dimension named above; each array names one. Nothing has to cross between parts.
All inputs are finite; a program needn't handle non-finite values.
Results may differ from a plain program's by a relative error of at most 0.007.
Values may be sent and summed in bfloat16 or wider, within the bound.
A program may use at most 64 MiB of HBM per device.

v0:
```python
import jax
import jax.numpy as jnp
from jax import lax
from jax.sharding import PartitionSpec as P

LAMBDA = 0.0051


def normalize(values):
    floats = values.astype(jnp.float32)
    center = jnp.mean(floats, axis=0, keepdims=True)
    spread = jnp.mean((floats - center) ** 2, axis=0, keepdims=True)
    inverse = lax.rsqrt(spread + 1e-05)
    return (((floats - center) * inverse).astype(jnp.bfloat16), inverse)


def backward(dnorm, normed, inverse):
    floats = normed.astype(jnp.float32)
    mean_d = jnp.mean(dnorm, axis=0, keepdims=True)
    mean_p = jnp.mean(dnorm * floats, axis=0, keepdims=True)
    return ((dnorm - mean_d - floats * mean_p) * inverse).astype(jnp.bfloat16)


def inner_matrix(normed):
    return lax.dot_general(
        normed, normed, (((1,), (1,)), ((), ())), preferred_element_type=jnp.float32
    )


def body(view_a, view_b):
    local_a, local_b = (
        lax.all_to_all(view_a, "feat", split_axis=1, concat_axis=0, tiled=True),
        lax.all_to_all(view_b, "feat", split_axis=1, concat_axis=0, tiled=True),
    )
    norm_a, inv_a = normalize(local_a)
    norm_b, inv_b = normalize(local_b)
    images = norm_a.shape[0]
    diag_corr = (
        jnp.sum(norm_a.astype(jnp.float32) * norm_b.astype(jnp.float32), axis=0, keepdims=True)
        / images
    )
    self_weight = -2.0 * (1.0 - diag_corr) - 2.0 * LAMBDA * diag_corr
    part_a = inner_matrix(norm_a)
    part_b = inner_matrix(norm_b)
    gram_a, gram_b = lax.psum((part_a, part_b), "feat")
    factor = 2.0 * LAMBDA / images
    mix_a = (gram_a * factor).astype(jnp.bfloat16)
    mix_b = (gram_b * factor).astype(jnp.bfloat16)
    dnorm_a = (
        jnp.dot(mix_b, norm_a, preferred_element_type=jnp.float32)
        + norm_b.astype(jnp.float32) * self_weight
    )
    dnorm_b = (
        jnp.dot(mix_a, norm_b, preferred_element_type=jnp.float32)
        + norm_a.astype(jnp.float32) * self_weight
    )
    grad_a = backward(dnorm_a, norm_a, inv_a)
    grad_b = backward(dnorm_b, norm_b, inv_b)
    return (
        lax.all_to_all(grad_a, "feat", split_axis=0, concat_axis=1, tiled=True),
        lax.all_to_all(grad_b, "feat", split_axis=0, concat_axis=1, tiled=True),
    )


def solution(mesh):
    placed = (P(("rep", "feat"), None), P(("rep", "feat"), None))
    return jax.shard_map(
        body,
        mesh=mesh,
        in_specs=placed,
        out_specs=(P(("rep", "feat"), None), P(("rep", "feat"), None)),
        check_vma=False,
    )
```

profile of v0, /device:TPU:0, one launch (start us, length us, event | category | flops | bytes accessed | tf_op | source)
XLA Modules:
  0.0 190.4 jit_solution(2214274792554007137)
XLA Ops:
  7.2 1.9 copy.15
  9.0 0.0 copy-start
  9.0 7.5 %all-to-all-start = ((bf16[16,16,1024]{2,0,1:T(8,128)(2,1)}), bf16[16,16,1024]{2,0,1:T(8,128)(2,1)S(1)}, u32[]{:S(2)}, u32[]{:S(2)}) async-start(bf16[16,16,1024]{2,0,1:T(8,128)(2,1)} %bitcast.49), calls=%async_computation | async-start | bytes 1048576 | tf_op jit(solution)/shard_map/all_to_all | solution.py:33
  16.6 0.0 copy-done
  16.6 0.8 copy.14
  17.4 13.6 %all-to-all-done = bf16[16,16,1024]{2,0,1:T(8,128)(2,1)S(1)} async-done(((bf16[16,16,1024]{2,0,1:T(8,128)(2,1)}), bf16[16,16,1024]{2,0,1:T(8,128)(2,1)S(1)}, u32[]{:S(2)}, u32[]{:S(2)}) %all-to-all-start) | async-done | bytes 524320 | tf_op jit(solution)/shard_map/all_to_all | solution.py:33
  31.0 4.1 %all-to-all-start.1 = ((bf16[16,16,1024]{2,0,1:T(8,128)(2,1)}), bf16[16,16,1024]{2,0,1:T(8,128)(2,1)S(1)}, u32[]{:S(2)}, u32[]{:S(2)}) async-start(bf16[16,16,1024]{2,0,1:T(8,128)(2,1)} %bitcast.48), calls=%async_computation.1 | async-start | bytes 1048576 | tf_op jit(solution)/shard_map/all_to_all | solution.py:32
  35.1 0.0 all-reduce.3.cloned.1.call-start
  35.2 0.1 convert_reduce_fusion.1
  35.3 0.2 multiply_reduce_fusion.2
  35.5 14.1 %all-to-all-done.1 = bf16[16,16,1024]{2,0,1:T(8,128)(2,1)S(1)} async-done(((bf16[16,16,1024]{2,0,1:T(8,128)(2,1)}), bf16[16,16,1024]{2,0,1:T(8,128)(2,1)S(1)}, u32[]{:S(2)}, u32[]{:S(2)}) %all-to-all-start.1) | async-done | bytes 524320 | tf_op jit(solution)/shard_map/all_to_all | solution.py:32
  49.6 0.1 convert_reduce_fusion
  49.7 0.2 multiply_reduce_fusion.1
  49.9 0.3 multiply_reduce_fusion
  50.2 1.0 fusion.18
  51.3 1.0 fusion.19
  52.3 0.0 all-reduce.3.cloned.1.call-update
  52.3 0.1 fusion.9
  52.5 0.1 fusion.11
  52.6 89.2 %all-reduce.3.cloned.1.call-done = (f32[256,256]{1,0:T(8,128)}, f32[256,256]{1,0:T(8,128)}) async-done(((f32[256,256]{1,0:T(8,128)}, f32[256,256]{1,0:T(8,128)}), (f32[256,256]{1,0:T(8,128)}, f32[256,256]{1,0:T(8,128)})) %all-reduce.3.cloned.1.call-update) | async-done | bytes 524304 | tf_op jit(solution)/shard_map/psum | solution.py:45
  141.9 1.3 fusion.16
  143.2 1.1 fusion.3
  144.3 0.0 copy-start.1
  144.3 5.4 %all-to-all-start.3 = ((bf16[16,16,1024]{2,1,0:T(8,128)(2,1)}), bf16[16,16,1024]{2,1,0:T(8,128)(2,1)S(1)}, u32[]{:S(2)}, u32[]{:S(2)}) async-start(bf16[16,16,1024]{2,1,0:T(8,128)(2,1)} %bitcast.10), calls=%async_computation.3 | async-start | bytes 1048576 | tf_op jit(solution)/shard_map/all_to_all | solution.py:61
  149.7 0.0 copy-done.1
  149.7 0.4 fusion.17
  150.1 1.1 fusion.7
  151.2 13.0 %all-to-all-done.3 = bf16[16,16,1024]{2,1,0:T(8,128)(2,1)S(1)} async-done(((bf16[16,16,1024]{2,1,0:T(8,128)(2,1)}), bf16[16,16,1024]{2,1,0:T(8,128)(2,1)S(1)}, u32[]{:S(2)}, u32[]{:S(2)}) %all-to-all-start.3) | async-done | bytes 524320 | tf_op jit(solution)/shard_map/all_to_all | solution.py:61
  164.1 4.1 %all-to-all-start.2 = ((bf16[16,16,1024]{2,1,0:T(8,128)(2,1)}), bf16[16,16,1024]{2,1,0:T(8,128)(2,1)S(1)}, u32[]{:S(2)}, u32[]{:S(2)}) async-start(bf16[16,16,1024]{2,1,0:T(8,128)(2,1)} %bitcast.7), calls=%async_computation.2 | async-start | bytes 1048576 | tf_op jit(solution)/shard_map/all_to_all | solution.py:60
  168.2 0.8 copy.11
  169.1 13.6 %all-to-all-done.2 = bf16[16,16,1024]{2,1,0:T(8,128)(2,1)S(1)} async-done(((bf16[16,16,1024]{2,1,0:T(8,128)(2,1)}), bf16[16,16,1024]{2,1,0:T(8,128)(2,1)S(1)}, u32[]{:S(2)}, u32[]{:S(2)}) %all-to-all-start.2) | async-done | bytes 524320 | tf_op jit(solution)/shard_map/all_to_all | solution.py:60
  182.7 0.8 copy.10
  (7 shorter events, 0.0 us)
Async XLA Ops:
  9.0 7.5 %copy-start = (bf16[16,16384]{1,0:T(8,128)(2,1)S(1)}, bf16[16,16384]{1,0:T(8,128)(2,1)}, u32[]{:S(2)}) copy-start(bf16[16,16384]{1,0:T(8,128)(2,1)} %param.2) | copy-start | bytes 1572868
  9.0 22.0 %all-to-all-start = ((bf16[16,16,1024]{2,0,1:T(8,128)(2,1)}), bf16[16,16,1024]{2,0,1:T(8,128)(2,1)S(1)}, u32[]{:S(2)}, u32[]{:S(2)}) async-start(bf16[16,16,1024]{2,0,1:T(8,128)(2,1)} %bitcast.49), calls=%async_computation | async-start | bytes 1048576 | tf_op jit(solution)/shard_map/all_to_all | solution.py:33
  31.0 18.6 %all-to-all-start.1 = ((bf16[16,16,1024]{2,0,1:T(8,128)(2,1)}), bf16[16,16,1024]{2,0,1:T(8,128)(2,1)S(1)}, u32[]{:S(2)}, u32[]{:S(2)}) async-start(bf16[16,16,1024]{2,0,1:T(8,128)(2,1)} %bitcast.48), calls=%async_computation.1 | async-start | bytes 1048576 | tf_op jit(solution)/shard_map/all_to_all | solution.py:32
  35.1 106.7 %all-reduce.3.cloned.1.call-start = ((), (), s32[]{:S(2)}) async-start(), calls=%async_computation.4 | async-start | bytes 1048576 | tf_op jit(solution)/shard_map/psum | solution.py:45
  144.3 5.4 %copy-start.1 = (f32[256,256]{1,0:T(8,128)S(1)}, f32[256,256]{1,0:T(8,128)}, u32[]{:S(2)}) copy-start(f32[256,256]{1,0:T(8,128)} %get-tuple-element.6) | copy-start | bytes 786436
  144.3 19.8 %all-to-all-start.3 = ((bf16[16,16,1024]{2,1,0:T(8,128)(2,1)}), bf16[16,16,1024]{2,1,0:T(8,128)(2,1)S(1)}, u32[]{:S(2)}, u32[]{:S(2)}) async-start(bf16[16,16,1024]{2,1,0:T(8,128)(2,1)} %bitcast.10), calls=%async_computation.3 | async-start | bytes 1048576 | tf_op jit(solution)/shard_map/all_to_all | solution.py:61
  164.1 18.6 %all-to-all-start.2 = ((bf16[16,16,1024]{2,1,0:T(8,128)(2,1)}), bf16[16,16,1024]{2,1,0:T(8,128)(2,1)S(1)}, u32[]{:S(2)}, u32[]{:S(2)}) async-start(bf16[16,16,1024]{2,1,0:T(8,128)(2,1)} %bitcast.7), calls=%async_computation.2 | async-start | bytes 1048576 | tf_op jit(solution)/shard_map/all_to_all | solution.py:60
Sparse Core Ops, SparseCore 0:
  52.5 89.3 all-reduce.2
where the time goes:
time: 191 us; the launch traced here: 190 us
  waiting for transfers between devices  144 us (75%)
  starting transfers between devices  21.1 us (11%)
  between operations  14.1 us (7%)
  local copies, waits for them, and re-layouts  4.38 us (2%)
  matrix products  3.8 us (2%)
  other arithmetic  3.29 us (2%)
    psum x1, waiting for transfers between devices, body(): gram_a, gram_b = lax.psum((part_a, part_b), 'feat')  89.2 us
    all_to_all x1, waiting for transfers between devices, body(): lax.all_to_all(view_a, 'feat', split_axis=1, concat_axis=0, tiled=True)  14.1 us
    all_to_all x1, waiting for transfers between devices, body(): lax.all_to_all(grad_a, 'feat', split_axis=0, concat_axis=1, tiled=True)  13.6 us
    all_to_all x1, waiting for transfers between devices, body(): lax.all_to_all(view_b, 'feat', split_axis=1, concat_axis=0, tiled=True)  13.6 us
    all_to_all x1, waiting for transfers between devices, body(): lax.all_to_all(grad_b, 'feat', split_axis=0, concat_axis=1, tiled=True)  13 us
    all_to_all x1, starting transfers between devices, body(): lax.all_to_all(view_b, 'feat', split_axis=1, concat_axis=0, tiled=True)  7.52 us
    all_to_all x1, starting transfers between devices, body(): lax.all_to_all(grad_b, 'feat', split_axis=0, concat_axis=1, tiled=True)  5.37 us
    all_to_all x1, starting transfers between devices, body(): lax.all_to_all(grad_a, 'feat', split_axis=0, concat_axis=1, tiled=True)  4.1 us
  transfers between devices with their start and end apart: 5, of which 5 were waited for; matrix products, arithmetic and copies ran while one was open for 2% of the time, Pallas kernels for 0%

commit v1 on v0

v1 whole, which is shorter than its diff:
```python
import functools

import jax
import jax.numpy as jnp
from jax import lax
from jax.experimental import pallas as pl
from jax.experimental.pallas import tpu as pltpu
from jax.sharding import PartitionSpec as P

LAMBDA = 0.0051
CHUNKS = 2


def kernel(n, chunks, view_a, view_b, out_a, out_b,
           recv, norm, inv, weight, part, terms, mix, grad,
           in_send, in_recv, own_sem, rs_send, rs_recv, ag_send, ag_recv, out_send, out_recv):
    me = lax.axis_index("feat")
    views, outs = (view_a, view_b), (out_a, out_b)
    rows, features = view_a.shape
    images = rows * n
    width = features // n
    step = width // chunks
    far = n // 2

    def my_rows(index):
        return pl.ds(pl.multiple_of(index * rows, rows), rows)

    def columns(index, chunk):
        return pl.ds(pl.multiple_of(index * width + chunk * step, 128), step)

    def each_peer(visit):
        def at(j, carry):
            offset = far + (j + 1) // 2 * (1 - 2 * (j % 2))
            visit(offset, lax.rem(me + offset, n))
            return carry
        lax.fori_loop(0, n - 1, at, 0)

    def push(src, dst, send, receive, peer):
        pltpu.make_async_remote_copy(
            src_ref=src, dst_ref=dst, send_sem=send, recv_sem=receive,
            device_id={"feat": peer}, device_id_type=pl.DeviceIdType.MESH,
        ).start()

    def await_bytes(ref, sem):
        pltpu.make_async_copy(ref, ref, sem).wait()

    barrier = pltpu.get_barrier_semaphore()
    each_peer(lambda offset, peer: pl.semaphore_signal(
        barrier, inc=1, device_id={"feat": peer}, device_id_type=pl.DeviceIdType.MESH))
    own = [[pltpu.make_async_copy(views[v].at[:, columns(me, c)], recv.at[v, c, my_rows(me)], own_sem.at[v, c])
            for c in range(chunks)] for v in range(2)]
    for v in range(2):
        for c in range(chunks):
            own[v][c].start()
    pl.semaphore_wait(barrier, n - 1)

    for v in range(2):
        for c in range(chunks):
            each_peer(lambda offset, peer: push(
                views[v].at[:, columns(peer, c)], recv.at[v, c, my_rows(me)],
                in_send.at[v, c], in_recv.at[v, c], peer))

    def normalize(v, c):
        own[v][c].wait()
        await_bytes(recv.at[v, c, pl.ds(0, images - rows)], in_recv.at[v, c])
        floats = recv[v, c].astype(jnp.float32)
        center = jnp.mean(floats, axis=0, keepdims=True)
        shifted = floats - center
        spread = jnp.mean(shifted * shifted, axis=0, keepdims=True)
        inverse = lax.rsqrt(spread + 1e-05)
        inv[v, c] = inverse
        norm[v, c] = (shifted * inverse).astype(jnp.bfloat16)

    def inner(v):
        total = None
        for c in range(chunks):
            term = lax.dot_general(norm[v, c], norm[v, c], (((1,), (1,)), ((), ())),
                                   preferred_element_type=jnp.float32)
            total = term if total is None else total + term
        part[v] = total.astype(jnp.bfloat16)
        each_peer(lambda offset, peer: push(
            part.at[v, my_rows(peer)], terms.at[v, offset - 1], rs_send.at[v], rs_recv.at[v], peer))

    def reduce(v):
        await_bytes(terms.at[v], rs_recv.at[v])
        total = part[v, my_rows(me)].astype(jnp.float32)
        for k in range(n - 1):
            total = total + terms[v, k].astype(jnp.float32)
        factor = 2.0 * LAMBDA / images
        mix[v, my_rows(me)] = (total * factor).astype(jnp.bfloat16)
        each_peer(lambda offset, peer: push(
            mix.at[v, my_rows(me)], mix.at[v, my_rows(me)], ag_send.at[v], ag_recv.at[v], peer))

    def self_weight(c):
        first, second = norm[0, c].astype(jnp.float32), norm[1, c].astype(jnp.float32)
        diagonal = jnp.sum(first * second, axis=0, keepdims=True) / images
        weight[c] = -2.0 * (1.0 - diagonal) - 2.0 * LAMBDA * diagonal

    def await_mix(v):
        await_bytes(mix.at[v, pl.ds(0, images - rows)], ag_recv.at[v])

    def backward(v, c):
        floats = norm[v, c].astype(jnp.float32)
        dnorm = jnp.dot(mix[1 - v], norm[v, c], preferred_element_type=jnp.float32)
        dnorm = dnorm + norm[1 - v, c].astype(jnp.float32) * weight[c]
        mean_d = jnp.mean(dnorm, axis=0, keepdims=True)
        mean_p = jnp.mean(dnorm * floats, axis=0, keepdims=True)
        grad[v, c] = ((dnorm - mean_d - floats * mean_p) * inv[v, c]).astype(jnp.bfloat16)
        each_peer(lambda offset, peer: push(
            grad.at[v, c, my_rows(peer)], outs[v].at[:, columns(me, c)],
            out_send.at[v, c], out_recv.at[v, c], peer))
        copy = pltpu.make_async_copy(grad.at[v, c, my_rows(me)], outs[v].at[:, columns(me, c)], own_sem.at[v, c])
        copy.start()
        return copy

    for c in range(chunks):
        normalize(0, c)
    inner(0)
    copies = []
    for c in range(chunks):
        normalize(1, c)
        self_weight(c)
        if c == 0:
            reduce(0)
    inner(1)
    await_mix(0)
    for c in range(chunks):
        copies.append(backward(1, c))
        if c == 0:
            reduce(1)
    await_mix(1)
    for c in range(chunks):
        copies.append(backward(0, c))

    for copy in copies:
        copy.wait()
    for v in range(2):
        await_bytes(terms.at[v], rs_send.at[v])
        await_bytes(mix.at[v, pl.ds(0, images - rows)], ag_send.at[v])
        for c in range(chunks):
            await_bytes(recv.at[v, c, pl.ds(0, images - rows)], in_send.at[v, c])
            await_bytes(grad.at[v, c, pl.ds(0, images - rows)], out_send.at[v, c])
            await_bytes(grad.at[v, c, pl.ds(0, images - rows)], out_recv.at[v, c])


def body(n, view_a, view_b):
    rows, features = view_a.shape
    images, width = rows * n, features // n
    chunks = CHUNKS
    while width % (chunks * 128):
        chunks -= 1
    step = width // chunks
    half = jnp.bfloat16
    blocks = (2, chunks, images, step)
    return pl.pallas_call(
        functools.partial(kernel, n, chunks),
        out_shape=[jax.ShapeDtypeStruct(view_a.shape, half)] * 2,
        in_specs=[pl.BlockSpec(memory_space=pl.ANY)] * 2,
        out_specs=[pl.BlockSpec(memory_space=pl.ANY)] * 2,
        scratch_shapes=[
            pltpu.VMEM(blocks, half),
            pltpu.VMEM(blocks, half),
            pltpu.VMEM((2, chunks, 1, step), jnp.float32),
            pltpu.VMEM((chunks, 1, step), jnp.float32),
            pltpu.VMEM((2, images, images), half),
            pltpu.VMEM((2, n - 1, rows, images), half),
            pltpu.VMEM((2, images, images), half),
            pltpu.VMEM(blocks, half),
            pltpu.SemaphoreType.DMA((2, chunks)),
            pltpu.SemaphoreType.DMA((2, chunks)),
            pltpu.SemaphoreType.DMA((2, chunks)),
            pltpu.SemaphoreType.DMA((2,)),
            pltpu.SemaphoreType.DMA((2,)),
            pltpu.SemaphoreType.DMA((2,)),
            pltpu.SemaphoreType.DMA((2,)),
            pltpu.SemaphoreType.DMA((2, chunks)),
            pltpu.SemaphoreType.DMA((2, chunks)),
        ],
        compiler_params=pltpu.CompilerParams(
            collective_id=0, has_side_effects=True, vmem_limit_bytes=48 * 1024 * 1024),
        cost_estimate=pl.CostEstimate(
            flops=8 * images * images * width, bytes_accessed=8 * rows * features, transcendentals=2 * width),
    )(view_a, view_b)


def solution(mesh):
    placed = (P(("rep", "feat"), None), P(("rep", "feat"), None))
    return jax.shard_map(
        functools.partial(body, mesh.shape["feat"]),
        mesh=mesh,
        in_specs=placed,
        out_specs=placed,
        check_vma=False,
    )
```

time: 191 us -> 71.1 us (0.37)
  waiting for transfers between devices: 144 us -> 0 us
  Pallas kernels: 0 us -> 66.6 us
  starting transfers between devices: 21.1 us -> 0 us
  between operations: 14.1 us -> 0.65 us
  matrix products: 3.8 us -> 0 us
  other arithmetic: 3.29 us -> 0 us
    psum x1 -> x0, waiting for transfers between devices: 89.2 us -> none  [body(): gram_a, gram_b = lax.psum((part_a, part_b), 'feat')]
    pallas_call x0 -> x1, Pallas kernels: none -> 66.6 us  [body(): pl.pallas_call(functools.partial(kernel, n, chunks), out_shape=[jax.Shape...]
    all_to_all x4 -> x0, waiting for transfers between devices: 54.4 us -> none  [the longest x1 14.1 us: body(): lax.all_to_all(view_a, 'feat', split_axis=1, concat_axis=0, tiled=True)]
    all_to_all x4 -> x0, starting transfers between devices: 21.1 us -> none  [the longest x1 7.52 us: body(): lax.all_to_all(view_b, 'feat', split_axis=1, concat_axis=0, tiled=True)]
    all_to_all x4 -> x0, local copies, waits for them, and re-layouts: 4.37 us -> none  [the longest x1 1.88 us: body(): lax.all_to_all(view_b, 'feat', split_axis=1, concat_axis=0, tiled=True)]
    dot_general x4 -> x0, matrix products: 3.8 us -> none  [the longest x2 2.08 us: inner_matrix(): lax.dot_general(normed, normed, (((1,), (1,)), ((), ())), preferred_eleme...]
    unnamed x4 -> x6, local copies, waits for them, and re-layouts: 0.01 us -> 3.66 us
    convert_element_type x4 -> x0, other arithmetic: 2.39 us -> none  [the longest x2 2.12 us: backward(): return ((dnorm - mean_d - floats * mean_p) * inverse).astype(jnp.bfloat16)]
  transfers between devices with their start and end apart: 5 -> 0, of which waited for: 5 -> 0; matrix products, arithmetic and copies ran while one was open for 2% -> 0% of each run, Pallas kernels for 0% -> 0%
where the time goes in v1:
time: 71.1 us; the launch traced here: 70.9 us
  Pallas kernels  66.6 us (94%)
  local copies, waits for them, and re-layouts  3.66 us (5%)
    pallas_call x1, Pallas kernels, body(): pl.pallas_call(functools.partial(kernel, n, chunks), out_shape=[jax.Shape...  66.6 us
    unnamed x6, local copies, waits for them, and re-layouts  3.66 us

profile of v1, /device:TPU:0, one launch (start us, length us, event | category | flops | bytes accessed | tf_op | source)
XLA Modules:
  0.0 70.9 jit_solution(10565412757700608492)
XLA Ops:
  0.6 0.0 copy-start
  0.6 1.0 %copy-done = bf16[16,16384]{1,0:T(8,128)(2,1)S(1)} copy-done((bf16[16,16384]{1,0:T(8,128)(2,1)S(1)}, bf16[16,16384]{1,0:T(8,128)(2,1)}, u32[]{:S(2)}) %copy-start) | copy-done | bytes 524312
  1.7 0.0 copy-start.1
  1.7 1.0 %copy-done.1 = bf16[16,16384]{1,0:T(8,128)(2,1)S(1)} copy-done((bf16[16,16384]{1,0:T(8,128)(2,1)S(1)}, bf16[16,16384]{1,0:T(8,128)(2,1)}, u32[]{:S(2)}) %copy-start.1) | copy-done | bytes 524312
  2.7 66.6 %shard_map.41 = (bf16[16,16384]{1,0:T(8,128)(2,1)S(1)}, bf16[16,16384]{1,0:T(8,128)(2,1)S(1)}) custom-call(bf16[16,16384]{1,0:T(8,128)(2,1)S(1)} %copy-done, bf16[16,16384]{1,0:T(8,128)(2,1)S(1)} %copy-done.1), custom_call_target="tpu_custom_call" | custom-call | flops 536870912 | bytes 2097152 | tf_op jit(solution)/shard_map/pallas_call | solution.py:155
  69.3 0.8 %copy.6 = bf16[16,16384]{1,0:T(8,128)(2,1)} copy(bf16[16,16384]{1,0:T(8,128)(2,1)S(1)} %get-tuple-element.4) | data formatting | bytes 1048576
  70.1 0.8 %copy.7 = bf16[16,16384]{1,0:T(8,128)(2,1)} copy(bf16[16,16384]{1,0:T(8,128)(2,1)S(1)} %get-tuple-element.5) | data formatting | bytes 1048576
Async XLA Ops:
  0.6 1.0 %copy-start = (bf16[16,16384]{1,0:T(8,128)(2,1)S(1)}, bf16[16,16384]{1,0:T(8,128)(2,1)}, u32[]{:S(2)}) copy-start(bf16[16,16384]{1,0:T(8,128)(2,1)} %view_a.1) | copy-start | bytes 1572868
  1.7 1.0 %copy-start.1 = (bf16[16,16384]{1,0:T(8,128)(2,1)S(1)}, bf16[16,16384]{1,0:T(8,128)(2,1)}, u32[]{:S(2)}) copy-start(bf16[16,16384]{1,0:T(8,128)(2,1)} %view_b.1) | copy-start | bytes 1572868

commit v2 on v1

--- a/solution.py
+++ b/solution.py
@@ -12,15 +12,19 @@
 
 
 def kernel(n, chunks, view_a, view_b, out_a, out_b,
-           recv, norm, inv, weight, part, terms, mix, grad,
-           in_send, in_recv, own_sem, rs_send, rs_recv, ag_send, ag_recv, out_send, out_recv):
+           recv, norm, inv, weight, part, terms, summed, sent, crossed, mix, grad,
+           in_send, in_recv, own_sem, rs_send, rs_recv, cross_send, cross_recv, ag_send, ag_recv, out_send, out_recv):
     me = lax.axis_index("feat")
     views, outs = (view_a, view_b), (out_a, out_b)
     rows, features = view_a.shape
     images = rows * n
     width = features // n
     step = width // chunks
-    far = n // 2
+    half = n // 2
+    owned = images // half
+    place = lax.rem(me, half)
+    base = me - place
+    mirror = lax.rem(me + half, n)
 
     def my_rows(index):
         return pl.ds(pl.multiple_of(index * rows, rows), rows)
@@ -28,12 +32,24 @@
     def columns(index, chunk):
         return pl.ds(pl.multiple_of(index * width + chunk * step, 128), step)
 
-    def each_peer(visit):
+    def owned_rows(index):
+        return pl.ds(pl.multiple_of(index * owned, owned), owned)
+
+    def each_peer(visit, group=None):
         def at(j, carry):
-            offset = far + (j + 1) // 2 * (1 - 2 * (j % 2))
+            offset = j if group is None else 2 * j + 1 + group
             visit(offset, lax.rem(me + offset, n))
             return carry
-        lax.fori_loop(0, n - 1, at, 0)
+        if group is None:
+            lax.fori_loop(1, n, at, 0)
+        else:
+            lax.fori_loop(0, half - group, at, 0)
+
+    def each_near(visit):
+        def at(offset, carry):
+            visit(offset, lax.rem(place + offset, half))
+            return carry
+        lax.fori_loop(1, half, at, 0)
 
     def push(src, dst, send, receive, peer):
         pltpu.make_async_remote_copy(
@@ -54,11 +70,15 @@
             own[v][c].start()
     pl.semaphore_wait(barrier, n - 1)
 
-    for v in range(2):
-        for c in range(chunks):
-            each_peer(lambda offset, peer: push(
-                views[v].at[:, columns(peer, c)], recv.at[v, c, my_rows(me)],
-                in_send.at[v, c], in_recv.at[v, c], peer))
+    def send_view(v, c, group=None):
+        each_peer(lambda offset, peer: push(
+            views[v].at[:, columns(peer, c)], recv.at[v, c, my_rows(me)],
+            in_send.at[v, c], in_recv.at[v, c], peer), group)
+
+    def send_grad(v, c, group=None):
+        each_peer(lambda offset, peer: push(
+            grad.at[v, c, my_rows(peer)], outs[v].at[:, columns(me, c)],
+            out_send.at[v, c], out_recv.at[v, c], peer), group)
 
     def normalize(v, c):
         own[v][c].wait()
@@ -78,18 +98,25 @@
                                    preferred_element_type=jnp.float32)
             total = term if total is None else total + term
         part[v] = total.astype(jnp.bfloat16)
-        each_peer(lambda offset, peer: push(
-            part.at[v, my_rows(peer)], terms.at[v, offset - 1], rs_send.at[v], rs_recv.at[v], peer))
+        each_near(lambda offset, other: push(
+            part.at[v, owned_rows(other)], terms.at[v, offset - 1], rs_send.at[v], rs_recv.at[v], base + other))
 
     def reduce(v):
         await_bytes(terms.at[v], rs_recv.at[v])
-        total = part[v, my_rows(me)].astype(jnp.float32)
-        for k in range(n - 1):
+        total = part[v, owned_rows(place)].astype(jnp.float32)
+        for k in range(half - 1):
             total = total + terms[v, k].astype(jnp.float32)
+        summed[v] = total
+        sent[v] = total.astype(jnp.bfloat16)
+        push(sent.at[v], crossed.at[v], cross_send.at[v], cross_recv.at[v], mirror)
+
+    def finish(v):
+        await_bytes(crossed.at[v], cross_recv.at[v])
+        total = summed[v] + crossed[v].astype(jnp.float32)
         factor = 2.0 * LAMBDA / images
-        mix[v, my_rows(me)] = (total * factor).astype(jnp.bfloat16)
-        each_peer(lambda offset, peer: push(
-            mix.at[v, my_rows(me)], mix.at[v, my_rows(me)], ag_send.at[v], ag_recv.at[v], peer))
+        mix[v, owned_rows(place)] = (total * factor).astype(jnp.bfloat16)
+        each_near(lambda offset, other: push(
+            mix.at[v, owned_rows(place)], mix.at[v, owned_rows(place)], ag_send.at[v], ag_recv.at[v], base + other))
 
     def self_weight(c):
         first, second = norm[0, c].astype(jnp.float32), norm[1, c].astype(jnp.float32)
@@ -97,7 +124,7 @@
         weight[c] = -2.0 * (1.0 - diagonal) - 2.0 * LAMBDA * diagonal
 
     def await_mix(v):
-        await_bytes(mix.at[v, pl.ds(0, images - rows)], ag_recv.at[v])
+        await_bytes(mix.at[v, pl.ds(0, images - owned)], ag_recv.at[v])
 
     def backward(v, c):
         floats = norm[v, c].astype(jnp.float32)
@@ -106,37 +133,53 @@
         mean_d = jnp.mean(dnorm, axis=0, keepdims=True)
         mean_p = jnp.mean(dnorm * floats, axis=0, keepdims=True)
         grad[v, c] = ((dnorm - mean_d - floats * mean_p) * inv[v, c]).astype(jnp.bfloat16)
-        each_peer(lambda offset, peer: push(
-            grad.at[v, c, my_rows(peer)], outs[v].at[:, columns(me, c)],
-            out_send.at[v, c], out_recv.at[v, c], peer))
         copy = pltpu.make_async_copy(grad.at[v, c, my_rows(me)], outs[v].at[:, columns(me, c)], own_sem.at[v, c])
         copy.start()
         return copy
 
+    view_groups = [(c, group) for c in range(chunks) for group in range(2)]
+    for c in range(chunks):
+        send_view(0, c)
+    send_view(1, *view_groups[0])
     for c in range(chunks):
         normalize(0, c)
     inner(0)
-    copies = []
-    for c in range(chunks):
+    send_view(1, *view_groups[1])
+    reduce(0)
+    for group in view_groups[2:3]:
+        send_view(1, *group)
+    finish(0)
+    for group in view_groups[3:]:
+        send_view(1, *group)
+    normalize(1, 0)
+    self_weight(0)
+    await_mix(0)
+    copies = [backward(1, 0)]
+    send_grad(1, 0, 0)
+    for c in range(1, chunks):
         normalize(1, c)
         self_weight(c)
-        if c == 0:
-            reduce(0)
     inner(1)
-    await_mix(0)
-    for c in range(chunks):
+    send_grad(1, 0, 1)
+    for c in range(1, chunks):
         copies.append(backward(1, c))
-        if c == 0:
-            reduce(1)
+    reduce(1)
+    for c in range(1, chunks):
+        send_grad(1, c, 0)
+    finish(1)
+    for c in range(1, chunks):
+        send_grad(1, c, 1)
     await_mix(1)
     for c in range(chunks):
         copies.append(backward(0, c))
+        send_grad(0, c)
 
     for copy in copies:
         copy.wait()
     for v in range(2):
         await_bytes(terms.at[v], rs_send.at[v])
-        await_bytes(mix.at[v, pl.ds(0, images - rows)], ag_send.at[v])
+        await_bytes(sent.at[v], cross_send.at[v])
+        await_bytes(mix.at[v, pl.ds(0, images - owned)], ag_send.at[v])
         for c in range(chunks):
             await_bytes(recv.at[v, c, pl.ds(0, images - rows)], in_send.at[v, c])
             await_bytes(grad.at[v, c, pl.ds(0, images - rows)], out_send.at[v, c])
@@ -155,7 +198,7 @@
     return pl.pallas_call(
         functools.partial(kernel, n, chunks),
         out_shape=[jax.ShapeDtypeStruct(view_a.shape, half)] * 2,
-        in_specs=[pl.BlockSpec(memory_space=pl.ANY)] * 2,
+        in_specs=[pl.BlockSpec(memory_space=pltpu.HBM)] * 2,
         out_specs=[pl.BlockSpec(memory_space=pl.ANY)] * 2,
         scratch_shapes=[
             pltpu.VMEM(blocks, half),
@@ -163,12 +206,17 @@
             pltpu.VMEM((2, chunks, 1, step), jnp.float32),
             pltpu.VMEM((chunks, 1, step), jnp.float32),
             pltpu.VMEM((2, images, images), half),
-            pltpu.VMEM((2, n - 1, rows, images), half),
+            pltpu.VMEM((2, n // 2 - 1, 2 * rows, images), half),
+            pltpu.VMEM((2, 2 * rows, images), jnp.float32),
+            pltpu.VMEM((2, 2 * rows, images), half),
+            pltpu.VMEM((2, 2 * rows, images), half),
             pltpu.VMEM((2, images, images), half),
             pltpu.VMEM(blocks, half),
             pltpu.SemaphoreType.DMA((2, chunks)),
             pltpu.SemaphoreType.DMA((2, chunks)),
             pltpu.SemaphoreType.DMA((2, chunks)),
+            pltpu.SemaphoreType.DMA((2,)),
+            pltpu.SemaphoreType.DMA((2,)),
             pltpu.SemaphoreType.DMA((2,)),
             pltpu.SemaphoreType.DMA((2,)),
             pltpu.SemaphoreType.DMA((2,)),

time: 71.1 us -> 64.6 us (0.909)
  Pallas kernels: 66.6 us -> 60 us
    pallas_call x1, Pallas kernels: 66.6 us -> 60 us  [body(): pl.pallas_call(functools.partial(kernel, n, chunks), out_shape=[jax.Shape...]
where the time goes in v2:
time: 64.6 us; the launch traced here: 64.4 us
  Pallas kernels  60 us (93%)
  local copies, waits for them, and re-layouts  3.66 us (6%)
  between operations  0.65 us (1%)
    pallas_call x1, Pallas kernels, body(): pl.pallas_call(functools.partial(kernel, n, chunks), out_shape=[jax.Shape...  60 us
    unnamed x6, local copies, waits for them, and re-layouts  3.66 us

profile of v2, /device:TPU:0, one launch (start us, length us, event | category | flops | bytes accessed | tf_op | source)
XLA Modules:
  0.0 64.4 jit_solution(7111053696598431566)
XLA Ops:
  0.6 0.0 copy-start
  0.6 1.0 %copy-done = bf16[16,16384]{1,0:T(8,128)(2,1)S(1)} copy-done((bf16[16,16384]{1,0:T(8,128)(2,1)S(1)}, bf16[16,16384]{1,0:T(8,128)(2,1)}, u32[]{:S(2)}) %copy-start) | copy-done | bytes 524312
  1.7 0.0 copy-start.1
  1.7 1.0 %copy-done.1 = bf16[16,16384]{1,0:T(8,128)(2,1)S(1)} copy-done((bf16[16,16384]{1,0:T(8,128)(2,1)S(1)}, bf16[16,16384]{1,0:T(8,128)(2,1)}, u32[]{:S(2)}) %copy-start.1) | copy-done | bytes 524312
  2.7 60.0 %shard_map.41 = (bf16[16,16384]{1,0:T(8,128)(2,1)S(1)}, bf16[16,16384]{1,0:T(8,128)(2,1)S(1)}) custom-call(bf16[16,16384]{1,0:T(8,128)(2,1)S(1)} %copy-done, bf16[16,16384]{1,0:T(8,128)(2,1)S(1)} %copy-done.1), custom_call_target="tpu_custom_call" | custom-call | flops 536870912 | bytes 2097152 | tf_op jit(solution)/shard_map/pallas_call | solution.py:198
  62.8 0.8 %copy.6 = bf16[16,16384]{1,0:T(8,128)(2,1)} copy(bf16[16,16384]{1,0:T(8,128)(2,1)S(1)} %get-tuple-element.4) | data formatting | bytes 1048576
  63.6 0.8 %copy.7 = bf16[16,16384]{1,0:T(8,128)(2,1)} copy(bf16[16,16384]{1,0:T(8,128)(2,1)S(1)} %get-tuple-element.5) | data formatting | bytes 1048576
Async XLA Ops:
  0.6 1.0 %copy-start = (bf16[16,16384]{1,0:T(8,128)(2,1)S(1)}, bf16[16,16384]{1,0:T(8,128)(2,1)}, u32[]{:S(2)}) copy-start(bf16[16,16384]{1,0:T(8,128)(2,1)} %view_a.1) | copy-start | bytes 1572868
  1.7 1.0 %copy-start.1 = (bf16[16,16384]{1,0:T(8,128)(2,1)S(1)}, bf16[16,16384]{1,0:T(8,128)(2,1)}, u32[]{:S(2)}) copy-start(bf16[16,16384]{1,0:T(8,128)(2,1)} %view_b.1) | copy-start | bytes 1572868

commit v3 on v2

--- a/solution.py
+++ b/solution.py
@@ -9,10 +9,11 @@
 
 LAMBDA = 0.0051
 CHUNKS = 2
+GROUPS = 4
 
 
 def kernel(n, chunks, view_a, view_b, out_a, out_b,
-           recv, norm, inv, weight, part, terms, summed, sent, crossed, mix, grad,
+           recv, norm, inv, weight, gram, part, terms, summed, sent, crossed, mix, grad,
            in_send, in_recv, own_sem, rs_send, rs_recv, cross_send, cross_recv, ag_send, ag_recv, out_send, out_recv):
     me = lax.axis_index("feat")
     views, outs = (view_a, view_b), (out_a, out_b)
@@ -37,13 +38,13 @@
 
     def each_peer(visit, group=None):
         def at(j, carry):
-            offset = j if group is None else 2 * j + 1 + group
+            offset = j if group is None else GROUPS * j + 1 + group
             visit(offset, lax.rem(me + offset, n))
             return carry
         if group is None:
             lax.fori_loop(1, n, at, 0)
         else:
-            lax.fori_loop(0, half - group, at, 0)
+            lax.fori_loop(0, (n - 1 - group + GROUPS - 1) // GROUPS, at, 0)
 
     def each_near(visit):
         def at(offset, carry):
@@ -91,13 +92,14 @@
         inv[v, c] = inverse
         norm[v, c] = (shifted * inverse).astype(jnp.bfloat16)
 
-    def inner(v):
-        total = None
-        for c in range(chunks):
-            term = lax.dot_general(norm[v, c], norm[v, c], (((1,), (1,)), ((), ())),
-                                   preferred_element_type=jnp.float32)
-            total = term if total is None else total + term
-        part[v] = total.astype(jnp.bfloat16)
+    def inner(v, c):
+        term = lax.dot_general(norm[v, c], norm[v, c], (((1,), (1,)), ((), ())), preferred_element_type=jnp.float32)
+        if c:
+            term = gram[...] + term
+        if c < chunks - 1:
+            gram[...] = term
+            return
+        part[v] = term.astype(jnp.bfloat16)
         each_near(lambda offset, other: push(
             part.at[v, owned_rows(other)], terms.at[v, offset - 1], rs_send.at[v], rs_recv.at[v], base + other))
 
@@ -137,38 +139,42 @@
         copy.start()
         return copy
 
-    view_groups = [(c, group) for c in range(chunks) for group in range(2)]
-    for c in range(chunks):
-        send_view(0, c)
-    send_view(1, *view_groups[0])
-    for c in range(chunks):
-        normalize(0, c)
-    inner(0)
-    send_view(1, *view_groups[1])
+    copies = []
+    send_view(0, 0)
+    send_view(0, 1)
+    send_view(1, 0, 0)
+    send_view(1, 0, 1)
+    normalize(0, 0)
+    inner(0, 0)
+    normalize(0, 1)
+    inner(0, 1)
+    send_view(1, 0, 2)
+    send_view(1, 0, 3)
+    send_view(1, 1, 0)
     reduce(0)
-    for group in view_groups[2:3]:
-        send_view(1, *group)
+    send_view(1, 1, 1)
+    send_view(1, 1, 2)
     finish(0)
-    for group in view_groups[3:]:
-        send_view(1, *group)
+    send_view(1, 1, 3)
     normalize(1, 0)
+    inner(1, 0)
     self_weight(0)
     await_mix(0)
-    copies = [backward(1, 0)]
+    copies.append(backward(1, 0))
     send_grad(1, 0, 0)
-    for c in range(1, chunks):
-        normalize(1, c)
-        self_weight(c)
-    inner(1)
+    normalize(1, 1)
+    self_weight(1)
+    inner(1, 1)
     send_grad(1, 0, 1)
-    for c in range(1, chunks):
-        copies.append(backward(1, c))
+    send_grad(1, 0, 2)
     reduce(1)
-    for c in range(1, chunks):
-        send_grad(1, c, 0)
+    send_grad(1, 0, 3)
+    copies.append(backward(1, 1))
+    send_grad(1, 1, 0)
     finish(1)
-    for c in range(1, chunks):
-        send_grad(1, c, 1)
+    send_grad(1, 1, 1)
+    send_grad(1, 1, 2)
+    send_grad(1, 1, 3)
     await_mix(1)
     for c in range(chunks):
         copies.append(backward(0, c))
@@ -205,6 +211,7 @@
             pltpu.VMEM(blocks, half),
             pltpu.VMEM((2, chunks, 1, step), jnp.float32),
             pltpu.VMEM((chunks, 1, step), jnp.float32),
+            pltpu.VMEM((images, images), jnp.float32),
             pltpu.VMEM((2, images, images), half),
             pltpu.VMEM((2, n // 2 - 1, 2 * rows, images), half),
             pltpu.VMEM((2, 2 * rows, images), jnp.float32),

time: 64.6 us -> 62.9 us (0.974)
  Pallas kernels: 60 us -> 58.4 us
    pallas_call x1, Pallas kernels: 60 us -> 58.4 us  [body(): pl.pallas_call(functools.partial(kernel, n, chunks), out_shape=[jax.Shape...]
where the time goes in v3:
time: 62.9 us; the launch traced here: 62.7 us
  Pallas kernels  58.4 us (93%)
  local copies, waits for them, and re-layouts  3.66 us (6%)
  between operations  0.65 us (1%)
    pallas_call x1, Pallas kernels, body(): pl.pallas_call(functools.partial(kernel, n, chunks), out_shape=[jax.Shape...  58.4 us
    unnamed x6, local copies, waits for them, and re-layouts  3.66 us

profile of v3, /device:TPU:0, one launch (start us, length us, event | category | flops | bytes accessed | tf_op | source)
XLA Modules:
  0.0 62.7 jit_solution(18416835179162385800)
XLA Ops:
  0.6 0.0 copy-start
  0.6 1.0 %copy-done = bf16[16,16384]{1,0:T(8,128)(2,1)S(1)} copy-done((bf16[16,16384]{1,0:T(8,128)(2,1)S(1)}, bf16[16,16384]{1,0:T(8,128)(2,1)}, u32[]{:S(2)}) %copy-start) | copy-done | bytes 524312
  1.7 0.0 copy-start.1
  1.7 1.0 %copy-done.1 = bf16[16,16384]{1,0:T(8,128)(2,1)S(1)} copy-done((bf16[16,16384]{1,0:T(8,128)(2,1)S(1)}, bf16[16,16384]{1,0:T(8,128)(2,1)}, u32[]{:S(2)}) %copy-start.1) | copy-done | bytes 524312
  2.7 58.4 %shard_map.41 = (bf16[16,16384]{1,0:T(8,128)(2,1)S(1)}, bf16[16,16384]{1,0:T(8,128)(2,1)S(1)}) custom-call(bf16[16,16384]{1,0:T(8,128)(2,1)S(1)} %copy-done, bf16[16,16384]{1,0:T(8,128)(2,1)S(1)} %copy-done.1), custom_call_target="tpu_custom_call" | custom-call | flops 536870912 | bytes 2097152 | tf_op jit(solution)/shard_map/pallas_call | solution.py:204
  61.1 0.8 %copy.6 = bf16[16,16384]{1,0:T(8,128)(2,1)} copy(bf16[16,16384]{1,0:T(8,128)(2,1)S(1)} %get-tuple-element.4) | data formatting | bytes 1048576
  61.9 0.8 %copy.7 = bf16[16,16384]{1,0:T(8,128)(2,1)} copy(bf16[16,16384]{1,0:T(8,128)(2,1)S(1)} %get-tuple-element.5) | data formatting | bytes 1048576
Async XLA Ops:
  0.6 1.0 %copy-start = (bf16[16,16384]{1,0:T(8,128)(2,1)S(1)}, bf16[16,16384]{1,0:T(8,128)(2,1)}, u32[]{:S(2)}) copy-start(bf16[16,16384]{1,0:T(8,128)(2,1)} %view_a.1) | copy-start | bytes 1572868
  1.7 1.0 %copy-start.1 = (bf16[16,16384]{1,0:T(8,128)(2,1)S(1)}, bf16[16,16384]{1,0:T(8,128)(2,1)}, u32[]{:S(2)}) copy-start(bf16[16,16384]{1,0:T(8,128)(2,1)} %view_b.1) | copy-start | bytes 1572868

commit v4 on v3

--- a/solution.py
+++ b/solution.py
@@ -163,10 +163,10 @@
     copies.append(backward(1, 0))
     send_grad(1, 0, 0)
     normalize(1, 1)
-    self_weight(1)
     inner(1, 1)
     send_grad(1, 0, 1)
     send_grad(1, 0, 2)
+    self_weight(1)
     reduce(1)
     send_grad(1, 0, 3)
     copies.append(backward(1, 1))

time: 62.9 us -> 62.9 us (level)
  no operation moved by 1% of the time
where the time goes in v4:
time: 62.9 us; the launch traced here: 62.7 us
  Pallas kernels  58.4 us (93%)
  local copies, waits for them, and re-layouts  3.66 us (6%)
  between operations  0.65 us (1%)
    pallas_call x1, Pallas kernels, body(): pl.pallas_call(functools.partial(kernel, n, chunks), out_shape=[jax.Shape...  58.4 us
    unnamed x6, local copies, waits for them, and re-layouts  3.66 us

profile of v4, /device:TPU:0, one launch (start us, length us, event | category | flops | bytes accessed | tf_op | source)
XLA Modules:
  0.0 62.7 jit_solution(701900528648476910)
XLA Ops:
  0.6 0.0 copy-start
  0.6 1.0 %copy-done = bf16[16,16384]{1,0:T(8,128)(2,1)S(1)} copy-done((bf16[16,16384]{1,0:T(8,128)(2,1)S(1)}, bf16[16,16384]{1,0:T(8,128)(2,1)}, u32[]{:S(2)}) %copy-start) | copy-done | bytes 524312
  1.7 0.0 copy-start.1
  1.7 1.0 %copy-done.1 = bf16[16,16384]{1,0:T(8,128)(2,1)S(1)} copy-done((bf16[16,16384]{1,0:T(8,128)(2,1)S(1)}, bf16[16,16384]{1,0:T(8,128)(2,1)}, u32[]{:S(2)}) %copy-start.1) | copy-done | bytes 524312
  2.7 58.4 %shard_map.41 = (bf16[16,16384]{1,0:T(8,128)(2,1)S(1)}, bf16[16,16384]{1,0:T(8,128)(2,1)S(1)}) custom-call(bf16[16,16384]{1,0:T(8,128)(2,1)S(1)} %copy-done, bf16[16,16384]{1,0:T(8,128)(2,1)S(1)} %copy-done.1), custom_call_target="tpu_custom_call" | custom-call | flops 536870912 | bytes 2097152 | tf_op jit(solution)/shard_map/pallas_call | solution.py:204
  61.1 0.8 %copy.6 = bf16[16,16384]{1,0:T(8,128)(2,1)} copy(bf16[16,16384]{1,0:T(8,128)(2,1)S(1)} %get-tuple-element.4) | data formatting | bytes 1048576
  61.9 0.8 %copy.7 = bf16[16,16384]{1,0:T(8,128)(2,1)} copy(bf16[16,16384]{1,0:T(8,128)(2,1)S(1)} %get-tuple-element.5) | data formatting | bytes 1048576
Async XLA Ops:
  0.6 1.0 %copy-start = (bf16[16,16384]{1,0:T(8,128)(2,1)S(1)}, bf16[16,16384]{1,0:T(8,128)(2,1)}, u32[]{:S(2)}) copy-start(bf16[16,16384]{1,0:T(8,128)(2,1)} %view_a.1) | copy-start | bytes 1572868
  1.7 1.0 %copy-start.1 = (bf16[16,16384]{1,0:T(8,128)(2,1)S(1)}, bf16[16,16384]{1,0:T(8,128)(2,1)}, u32[]{:S(2)}) copy-start(bf16[16,16384]{1,0:T(8,128)(2,1)} %view_b.1) | copy-start | bytes 1572868
